TPU v7x, 256 devices: a whole 4x4x8 slice. The times are simulated.
256 devices in a mesh: box: 64 (over x, z, core), col: 4 (over y).
Axes of the slice: x: 4, y: 4, z: 8, core: 2. Of those that a mesh axis runs over, the one named last changes fastest.
Arguments:
- leaf_maps: float32 [64, 1024, 1024], P('box', None, 'col'), may hold values from -0.08385255 to 0.08385255
- interface_blocks: int32 [3, 64, 4], replicated, may hold values from 0 to 7, as said below
- root_data: float32 [8, 1024, 512], P(None, None, 'col'), may hold values from -6 to 6
Outputs:
- leaf_data: float32 [64, 1024, 512], P('box', None, 'col')
Inputs may be any that keep to these rules, and one draw needn't show every extreme that they name: `interface_blocks`: entry k of every list is block 2k or 2k+1.
All inputs are finite; a program needn't handle non-finite values.
Results may differ from a plain program's by a relative error of at most 0.0003.
Values sent between devices are 32-bit elements; how exact they have to be, the bound alone decides.
A program may use at most 128 MiB of HBM per device.

v0:
```python
import jax
import jax.numpy as jnp
from jax import lax
from jax.sharding import PartitionSpec as P

LEVELS = 3
NEWTON = 2
IFACE = 512


def from_partner(block, axis, distance):
    count = lax.axis_size(axis)
    route = []
    for low in range(count):
        high = low | 1 << distance
        if high != low and high < count:
            route += [(low, high), (high, low)]
    return lax.ppermute(block, axis, route)


def high_dot(left, right):
    return jnp.dot(left, right, precision=lax.Precision.HIGHEST, preferred_element_type=jnp.float32)


def high_tdot(left, right):
    return lax.dot_general(
        left,
        right,
        (((0,), (0,)), ((), ())),
        precision=lax.Precision.HIGHEST,
        preferred_element_type=jnp.float32,
    )


def take_blocks(matrix, block_ids, along, block_width):
    if along == 0:
        shaped = matrix.reshape(matrix.shape[0] // block_width, block_width, matrix.shape[1])
        return jnp.take(shaped, block_ids, axis=0).reshape(-1, matrix.shape[1])
    shaped = matrix.reshape(matrix.shape[0], matrix.shape[1] // block_width, block_width)
    return jnp.take(shaped, block_ids, axis=1).reshape(matrix.shape[0], -1)


def own_block(local_map, ext_list, bits, shard, block_width):
    ext_rows = take_blocks(local_map, ext_list, 0, block_width)
    bit_here = lax.dynamic_index_in_dim(bits, shard, 0, keepdims=False)
    return lax.dynamic_slice_in_dim(ext_rows, (1 - bit_here) * block_width, block_width, 1)


def merged_columns(alpha_block, beta_block, operators, shard, block_width):
    (
        alpha_inner,
        beta_inner,
        coupling,
        alpha_outer,
        beta_outer,
        alpha_bit,
        beta_bit,
        alpha_ext,
        beta_ext,
    ) = operators
    coupling_beta = high_dot(coupling, beta_inner)
    alpha_own = lax.dynamic_slice_in_dim(alpha_outer, shard * block_width, block_width, 1)
    beta_own = lax.dynamic_slice_in_dim(beta_outer, shard * block_width, block_width, 1)
    alpha_cols = high_dot(coupling_beta, alpha_own)
    alpha_back = -(alpha_own + high_dot(alpha_inner, alpha_cols))
    beta_cols = -high_dot(coupling, beta_own)
    beta_back = -high_dot(alpha_inner, beta_cols)
    upper_rows = jnp.concatenate(
        [alpha_block + high_tdot(alpha_outer, alpha_cols), high_tdot(alpha_outer, beta_cols)], 1
    )
    lower_rows = jnp.concatenate(
        [high_tdot(beta_outer, alpha_back), beta_block + high_tdot(beta_outer, beta_back)], 1
    )
    pairs_count = upper_rows.shape[0] // block_width
    stacked = jnp.stack(
        [
            upper_rows.reshape(pairs_count, block_width, -1),
            lower_rows.reshape(pairs_count, block_width, -1),
        ],
        1,
    )
    return stacked.reshape(2 * upper_rows.shape[0], -1)


def place_blocks(far_data, near_data, bits, block_width):
    pairs_count = bits.shape[0]
    columns = far_data.shape[1]
    chooser = bits[:, None] == jnp.arange(2, dtype=jnp.int32)[None, :]
    shaped_far = far_data.reshape(pairs_count, 1, block_width, columns)
    shaped_near = near_data.reshape(pairs_count, 1, block_width, columns)
    return jnp.where(chooser[:, :, None, None], shaped_near, shaped_far).reshape(
        pairs_count * 2 * block_width, columns
    )


def descend(parent, operators, block_width):
    (
        alpha_inner,
        beta_inner,
        coupling,
        alpha_outer,
        beta_outer,
        alpha_bit,
        beta_bit,
        alpha_ext,
        beta_ext,
    ) = operators
    columns = parent.shape[1]
    split_rows = parent.reshape(alpha_bit.shape[0], 2, block_width, columns)
    alpha_far = split_rows[:, 0].reshape(-1, columns)
    beta_far = split_rows[:, 1].reshape(-1, columns)
    through = high_dot(alpha_outer, alpha_far)
    alpha_near = high_dot(coupling, high_dot(beta_inner, through) - high_dot(beta_outer, beta_far))
    beta_near = -(through + high_dot(alpha_inner, alpha_near))
    return (
        place_blocks(alpha_far, alpha_near, alpha_bit, block_width),
        place_blocks(beta_far, beta_near, beta_bit, block_width),
    )


def shards(leaf_maps, interface_blocks, root_data):
    position = lax.axis_index("box")
    shard = lax.axis_index("col")
    boxes = interface_blocks.shape[1]
    current = leaf_maps[0]
    block_width = current.shape[1] // 2
    offsets = 2 * jnp.arange(interface_blocks.shape[2], dtype=jnp.int32)
    identity = jnp.eye(IFACE, dtype=jnp.float32)
    stored = []
    for level_index in range(LEVELS):
        span = 2**level_index
        upper_half = position // span % 2 == 1
        alpha_node = position - position % (2 * span)
        beta_node = jnp.minimum(alpha_node + span, boxes - 1)
        table = interface_blocks[level_index]
        alpha_list = lax.dynamic_index_in_dim(table, alpha_node, 0, keepdims=False)
        beta_list = lax.dynamic_index_in_dim(table, beta_node, 0, keepdims=False)
        alpha_bit = alpha_list - offsets
        beta_bit = beta_list - offsets
        alpha_ext = offsets + 1 - alpha_bit
        beta_ext = offsets + 1 - beta_bit
        other = from_partner(current, "box", level_index)
        alpha_map = jnp.where(upper_half, other, current)
        beta_map = jnp.where(upper_half, current, other)
        alpha_local = take_blocks(alpha_map, alpha_list, 0, block_width)
        beta_local = take_blocks(beta_map, beta_list, 0, block_width)
        alpha_block = own_block(alpha_map, alpha_ext, alpha_bit, shard, block_width)
        beta_block = own_block(beta_map, beta_ext, beta_bit, shard, block_width)
        alpha_rows, beta_rows = (
            lax.all_gather(alpha_local, "col", axis=1, tiled=True),
            lax.all_gather(beta_local, "col", axis=1, tiled=True),
        )
        alpha_inner = take_blocks(alpha_rows, alpha_list, 1, block_width)
        alpha_outer = take_blocks(alpha_rows, alpha_ext, 1, block_width)
        beta_inner = take_blocks(beta_rows, beta_list, 1, block_width)
        beta_outer = take_blocks(beta_rows, beta_ext, 1, block_width)
        product = high_dot(beta_inner, alpha_inner)
        iterate = identity + product
        defect = identity - product
        for _ in range(NEWTON):
            iterate = 2.0 * iterate - high_dot(iterate, high_dot(defect, iterate))
        operators = (
            alpha_inner,
            beta_inner,
            iterate,
            alpha_outer,
            beta_outer,
            alpha_bit,
            beta_bit,
            alpha_ext,
            beta_ext,
        )
        stored.append(operators)
        if level_index + 1 < LEVELS:
            current = merged_columns(alpha_block, beta_block, operators, shard, block_width)
    group = position // 2**LEVELS
    data = lax.dynamic_index_in_dim(root_data, group, 0, keepdims=False)
    for level_index in reversed(range(LEVELS)):
        span = 2**level_index
        alpha_data, beta_data = descend(data, stored[level_index], block_width)
        upper_half = position // span % 2 == 1
        data = jnp.where(upper_half, beta_data, alpha_data)
    return data[None]


def solution(mesh):
    return jax.shard_map(
        shards,
        mesh=mesh,
        in_specs=(P("box", None, "col"), P(), P(None, None, "col")),
        out_specs=P("box", None, "col"),
        check_vma=False,
    )
```

profile of v0, /device:TPU:1, one launch (start us, length us, event | category | flops | bytes accessed | tf_op | source)
XLA Modules:
  0.0 519.3 jit_solution(12594467039067836324)
XLA Ops:
  6.5 3.2 collective-permute-start
  23.0 26.9 %all-gather.7.cloned.1.call-done = f32[512,1024]{0,1:T(8,128)} async-done(((f32[512,256]{0,1:T(8,128)}), f32[512,1024]{0,1:T(8,128)}) %all-gather.7.cloned.1.call-update) | async-done | bytes 2097168 | tf_op jit(solution)/shard_map/all_gather | solution.py:150
  54.0 31.2 %all-gather.9.cloned.1.call-done = f32[512,1024]{0,1:T(8,128)} async-done(((f32[512,256]{0,1:T(8,128)}), f32[512,1024]{0,1:T(8,128)}) %all-gather.9.cloned.1.call-update) | async-done | bytes 2097168 | tf_op jit(solution)/shard_map/all_gather | solution.py:151
  85.2 2.4 copy.19
  90.7 2.3 select_bitcast_fusion.11
  95.2 2.7 select_bitcast_fusion.10
  100.6 2.6 copy.20
  103.2 4.7 fusion.29
  116.7 2.5 convolution_negate_fusion.2
  121.2 2.8 fusion.30
  124.8 2.3 fusion.31
  127.1 2.8 fusion.4
  138.9 22.4 %collective-permute-done.1 = f32[1024,256]{1,0:T(8,128)} collective-permute-done((f32[1024,256]{1,0:T(8,128)S(1)}, f32[1024,256]{1,0:T(8,128)}, u32[]{:S(2)}, u32[]{:S(2)}) %collective-permute-start.1) | collective-permute-done | bytes 1048608 | tf_op jit(solution)/shard_map/ppermute | solution.py:18
  161.3 2.7 broadcast_select_fusion.3
  164.1 2.7 gather_fusion.8
  177.0 2.6 gather_fusion.15
  185.0 20.2 %all-gather.11.cloned.1.call-done = f32[512,1024]{0,1:T(8,128)} async-done(((f32[512,256]{0,1:T(8,128)}), f32[512,1024]{0,1:T(8,128)}) %all-gather.11.cloned.1.call-update) | async-done | bytes 2097168 | tf_op jit(solution)/shard_map/all_gather | solution.py:150
  205.2 2.9 copy.30
  208.1 2.2 gather_fusion.13
  210.3 3.2 gather_fusion.9
  213.5 26.8 %all-gather.13.cloned.1.call-done = f32[512,1024]{0,1:T(8,128)} async-done(((f32[512,256]{0,1:T(8,128)}), f32[512,1024]{0,1:T(8,128)}) %all-gather.13.cloned.1.call-update) | async-done | bytes 2097168 | tf_op jit(solution)/shard_map/all_gather | solution.py:151
  240.3 3.3 copy.34
  243.6 3.2 gather_fusion.14
  246.8 3.2 gather_fusion.12
  250.0 2.3 select_bitcast_fusion.7
  255.0 2.5 copy.31
  258.6 2.4 select_bitcast_fusion.6
  262.0 2.5 copy.40
  264.6 2.6 copy.35
  267.2 4.7 fusion.34
  279.6 2.3 convolution_negate_fusion.1
  281.9 2.5 convolution_negate_fusion
  286.3 2.8 fusion.35
  290.0 2.3 fusion.36
  292.3 3.5 fusion.3
  297.9 2.1 copy.59
  300.0 2.6 fusion.38
  302.6 2.2 convolution_add_fusion.3
  307.6 2.3 pad_maximum_fusion.1
  309.9 2.7 collective-permute-start.2
  312.6 45.5 %collective-permute-done.2 = f32[1024,256]{1,0:T(8,128)} collective-permute-done((f32[1024,256]{1,0:T(8,128)}, f32[1024,256]{1,0:T(8,128)}, u32[]{:S(2)}, u32[]{:S(2)}) %collective-permute-start.2) | collective-permute-done | bytes 1048608 | tf_op jit(solution)/shard_map/ppermute | solution.py:18
  358.0 3.0 broadcast_select_fusion.1
  361.0 2.6 gather_fusion.19
  367.7 2.6 gather_fusion.16
  372.2 2.0 copy.62
  376.8 25.4 %all-gather.17.cloned.1.call-done = f32[512,1024]{0,1:T(8,128)} async-done(((f32[512,256]{0,1:T(8,128)}), f32[512,1024]{0,1:T(8,128)}) %all-gather.17.cloned.1.call-update) | async-done | bytes 2097168 | tf_op jit(solution)/shard_map/all_gather | solution.py:151
  402.2 2.9 copy.50
  405.1 32.2 %all-gather.15.cloned.1.call-done = f32[512,1024]{0,1:T(8,128)} async-done(((f32[512,256]{0,1:T(8,128)}), f32[512,1024]{0,1:T(8,128)}) %all-gather.15.cloned.1.call-update) | async-done | bytes 2097168 | tf_op jit(solution)/shard_map/all_gather | solution.py:150
  437.3 2.9 copy.45
  440.2 3.2 gather_fusion.18
  443.4 3.2 gather_fusion.17
  446.6 2.3 select_bitcast_fusion.2
  448.9 2.5 copy.48
  451.4 2.3 select_bitcast_fusion.3
  453.8 2.5 copy.46
  456.3 3.2 gather_fusion.20
  459.5 3.2 gather_fusion.21
  462.7 2.4 select_bitcast_fusion.1
  466.3 2.5 copy.53
  468.8 2.5 copy.51
  471.4 3.2 fusion.39
  474.6 3.0 fusion.41
  477.6 3.5 fusion.40
  483.0 2.1 convolution_subtract_fusion.1
  (212 shorter events, 116.8 us)
Async XLA Ops:
  6.5 43.3 %all-gather.7.cloned.1.call-start = ((), (), s32[]{:S(2)}) async-start(), calls=%async_computation | async-start | bytes 2621440 | tf_op jit(solution)/shard_map/all_gather | solution.py:150
  6.5 5.7 %collective-permute-start = (f32[1024,256]{1,0:T(8,128)}, f32[1024,256]{1,0:T(8,128)S(1)}, u32[]{:S(2)}, u32[]{:S(2)}) collective-permute-start(f32[1024,256]{1,0:T(8,128)} %bitcast.261), channel_id=1, source_target_pairs={{0,4},{4,0},{8,12},{12,8},{16,20},{20,16},{24,28},{28,24},{32,36},... | collective-permute-start | bytes 3145736 | tf_op jit(solution)/shard_map/ppermute | solution.py:18
  15.4 69.8 %all-gather.9.cloned.1.call-start = ((), (), s32[]{:S(2)}) async-start(), calls=%async_computation.1 | async-start | bytes 2621440 | tf_op jit(solution)/shard_map/all_gather | solution.py:151
  17.2 188.0 %all-gather.11.cloned.1.call-start = ((), (), s32[]{:S(2)}) async-start(), calls=%async_computation.2 | async-start | bytes 2621440 | tf_op jit(solution)/shard_map/all_gather | solution.py:150
  93.5 4.4 copy-start.18
  95.2 34.7 %copy-start.2 = (f32[512,4,128]{0,2,1:T(8,128)}, f32[512,4,128]{0,2,1:T(8,128)S(1)}, u32[]{:S(2)}) copy-start(f32[512,4,128]{0,2,1:T(8,128)S(1)} %copy.16) | copy-start | bytes 3145732
  115.5 5.7 %copy-start.9 = (f32[512,512]{1,0:T(8,128)}, f32[512,512]{1,0:T(8,128)S(1)}, u32[]{:S(2)}) copy-start(f32[512,512]{1,0:T(8,128)S(1)} %convolution_subtract_fusion.4) | copy-start | bytes 3145732
  115.5 5.7 %copy-start.7 = (f32[512,4,128]{0,2,1:T(8,128)S(1)}, f32[512,4,128]{0,2,1:T(8,128)}, u32[]{:S(2)}) copy-start(f32[512,4,128]{0,2,1:T(8,128)} %copy.20) | copy-start | bytes 3145732
  124.8 5.1 copy-start.26
  127.1 4.1 copy-start.30
  131.2 2.3 copy-start.24
  131.2 2.3 copy-start.29
  137.1 24.2 %collective-permute-start.1 = (f32[1024,256]{1,0:T(8,128)S(1)}, f32[1024,256]{1,0:T(8,128)}, u32[]{:S(2)}, u32[]{:S(2)}) collective-permute-start(f32[1024,256]{1,0:T(8,128)S(1)} %bitcast.220), channel_id=1, source_target_pairs={{0,8},{8,0},{4,12},{12,4},{16,24},{24,16},{20,28},{28,20},{32,40},... | collective-permute-start | bytes 3145736 | tf_op jit(solution)/shard_map/ppermute | solution.py:18
  164.0 6.8 %copy-start.22 = (f32[1024,256]{1,0:T(8,128)S(1)}, f32[1024,256]{1,0:T(8,128)}, u32[]{:S(2)}) copy-start(f32[1024,256]{1,0:T(8,128)} %get-tuple-element.28) | copy-start | bytes 3145732
  170.7 69.6 %all-gather.13.cloned.1.call-start = ((), (), s32[]{:S(2)}) async-start(), calls=%async_computation.3 | async-start | bytes 2621440 | tf_op jit(solution)/shard_map/all_gather | solution.py:151
  174.4 7.2 %copy-start.21 = (f32[1024,256]{1,0:T(8,128)S(1)}, f32[1024,256]{1,0:T(8,128)}, u32[]{:S(2)}) copy-start(f32[1024,256]{1,0:T(8,128)} %get-tuple-element.27) | copy-start | bytes 3145732
  174.4 227.8 %all-gather.17.cloned.1.call-start = ((), (), s32[]{:S(2)}) async-start(), calls=%async_computation.5 | async-start | bytes 2621440 | tf_op jit(solution)/shard_map/all_gather | solution.py:151
  257.5 3.4 copy-start.17
  279.4 6.9 %copy-start.13 = (f32[512,512]{1,0:T(8,128)}, f32[512,512]{1,0:T(8,128)S(1)}, u32[]{:S(2)}) copy-start(f32[512,512]{1,0:T(8,128)S(1)} %convolution_subtract_fusion.2) | copy-start | bytes 3145732
  279.6 4.8 copy-start.4
  279.6 6.7 %copy-start.11 = (f32[512,4,128]{0,2,1:T(8,128)S(1)}, f32[512,4,128]{0,2,1:T(8,128)}, u32[]{:S(2)}) copy-start(f32[512,4,128]{0,2,1:T(8,128)} %copy.35) | copy-start | bytes 3145732
  290.0 5.8 %copy-start.5 = (f32[512,4,128]{0,2,1:T(8,128)S(1)}, f32[512,4,128]{0,2,1:T(8,128)}, u32[]{:S(2)}) copy-start(f32[512,4,128]{0,2,1:T(8,128)} %copy.31) | copy-start | bytes 3145732
  290.0 5.8 %copy-start.25 = (f32[512,128]{0,1:T(8,128)S(1)}, f32[512,128]{0,1:T(8,128)}, u32[]{:S(2)}) copy-start(f32[512,128]{0,1:T(8,128)} %copy.67) | copy-start | bytes 786436
  292.3 4.7 copy-start.31
  297.1 5.5 %copy-start.23 = (f32[512,128]{0,1:T(8,128)S(1)}, f32[512,128]{0,1:T(8,128)}, u32[]{:S(2)}) copy-start(f32[512,128]{0,1:T(8,128)} %copy.69) | copy-start | bytes 786436
  300.0 2.6 copy-start
  309.9 48.1 %collective-permute-start.2 = (f32[1024,256]{1,0:T(8,128)}, f32[1024,256]{1,0:T(8,128)}, u32[]{:S(2)}, u32[]{:S(2)}) collective-permute-start(f32[1024,256]{1,0:T(8,128)} %bitcast.42), channel_id=1, source_target_pairs={{0,16},{16,0},{4,20},{20,4},{8,24},{24,8},{12,28},{28,12},{32,48},... | collective-permute-start | bytes 3145736 | tf_op jit(solution)/shard_map/ppermute | solution.py:18
  367.6 69.7 %all-gather.15.cloned.1.call-start = ((), (), s32[]{:S(2)}) async-start(), calls=%async_computation.4 | async-start | bytes 2621440 | tf_op jit(solution)/shard_map/all_gather | solution.py:150
  462.7 2.4 copy-start.19
  471.4 6.3 %copy-start.15 = (f32[512,4,128]{0,2,1:T(8,128)S(1)}, f32[512,4,128]{0,2,1:T(8,128)}, u32[]{:S(2)}) copy-start(f32[512,4,128]{0,2,1:T(8,128)} %copy.48) | copy-start | bytes 3145732
  471.4 6.3 %copy-start.16 = (f32[512,4,128]{0,2,1:T(8,128)S(1)}, f32[512,4,128]{0,2,1:T(8,128)}, u32[]{:S(2)}) copy-start(f32[512,4,128]{0,2,1:T(8,128)} %copy.51) | copy-start | bytes 3145732
  487.0 1.9 copy-start.20
  487.0 1.9 copy-start.28
  490.7 2.8 copy-start.27
  491.7 2.1 copy-start.6
  493.5 2.1 copy-start.12
  493.7 3.8 copy-start.1
  495.6 3.9 copy-start.14
  500.5 2.1 copy-start.3
  502.3 2.1 copy-start.8
  504.4 3.6 copy-start.10
Sparse Core Ops, SparseCore 0:
  15.5 34.3 all-gather.6
  51.7 33.4 all-gather.8
  170.9 34.2 all-gather.10
  206.8 33.4 all-gather.12
  367.8 34.3 all-gather.16
  403.8 33.4 all-gather.14
where the time goes:
time: 524 us; the launch traced here: 519 us
  waiting for transfers between devices  232 us (44%)
  local copies, waits for them, and re-layouts  115 us (22%)
  matrix products  102 us (19%)
  other arithmetic  45.3 us (9%)
  between operations  17.4 us (3%)
  starting transfers between devices  7.44 us (1%)
    dot_general x40, matrix products, high_dot(): jnp.dot(left, right, precision=lax.Precision.HIGHEST, preferred_element_t...  88.1 us
    all_gather x3, waiting for transfers between devices, shards(): lax.all_gather(beta_local, 'col', axis=1, tiled=True)  83.4 us
    all_gather x3, waiting for transfers between devices, shards(): lax.all_gather(alpha_local, 'col', axis=1, tiled=True)  79.3 us
    ppermute x3, waiting for transfers between devices, from_partner(): return lax.ppermute(block, axis, route)  69.4 us
    gather x12, local copies, waits for them, and re-layouts, take_blocks(): return jnp.take(shaped, block_ids, axis=1).reshape(matrix.shape[0], -1)  29.9 us
    select_n x12, local copies, waits for them, and re-layouts, take_blocks(): return jnp.take(shaped, block_ids, axis=1).reshape(matrix.shape[0], -1)  25.5 us
    select_n x13, other arithmetic, take_blocks(): return jnp.take(shaped, block_ids, axis=1).reshape(matrix.shape[0], -1)  21.4 us
    reshape x6, local copies, waits for them, and re-layouts, take_blocks(): matrix.reshape(matrix.shape[0], matrix.shape[1] // block_width, block_width)  16.3 us
  transfers between devices with their start and end apart: 9, of which 9 were waited for; matrix products, arithmetic and copies ran while one was open for 9% of the time, Pallas kernels for 0%

commit v1 on v0

v1 whole, which is shorter than its diff:
```python
import functools

import jax
import jax.numpy as jnp
from jax import lax
from jax.experimental import pallas as pl
from jax.experimental.pallas import tpu as pltpu
from jax.sharding import PartitionSpec as P

LEVELS = 3
IFACE = 512
BLK = 128
HALF = 256
F32 = jnp.float32
BF16 = jnp.bfloat16
MESH = pl.DeviceIdType.MESH

ACROSS, RIGHT, LEFT, ON_RIGHT, ON_LEFT, SIBLING, COPIES = 0, 1, 3, 5, 6, 7, 15


def split(x):
    high = x.astype(BF16)
    return high, (x - high.astype(F32)).astype(BF16)


def mm(a, b):
    dot = functools.partial(jnp.dot, preferred_element_type=F32)
    return dot(a[0], b[0]) + (dot(a[0], b[1]) + dot(a[1], b[0]))


def pick(flag, yes, no):
    return jnp.where(jnp.broadcast_to(flag, yes.shape) == 1, yes, no)


def kernel(
    table, leaf, root, out,
    g0i, g0o, g1i, g1o, g2i, g2o,
    mats, work, wf, vs, ss, ext, dall, p, fs, t32, ts, ds,
    send_sem, recv_sem, ext_send, ext_recv, root_sem,
):
    pos = lax.axis_index("box")
    y = lax.axis_index("col")
    c = pos % 2
    gathered = ((g0i, g0o), (g1i, g1o), (g2i, g2o))
    slots = (y, (y + 3) % 4, (y + 1) % 4, (y + 2) % 4)
    right, left, sibling = (pos, slots[2]), (pos, slots[1]), (pos ^ 1, y)

    root_copy = pltpu.make_async_copy(root.at[pos // 8], p, root_sem)
    root_copy.start()

    barrier = pltpu.get_barrier_semaphore()
    for peer in (right, left, sibling, (pos ^ 2, y), (pos ^ 4, y)):
        pl.semaphore_signal(barrier, inc=1, device_id=peer, device_id_type=MESH)

    def own_map(level):
        return (pos >> level) & 1

    def bit_of(level, k):
        return table[level, pos - pos % 2**level, k] & 1

    def unit(level, phase, slot, u):
        g = gathered[level][phase]
        return g.at[slot, c, u] if level == 0 else g.at[slot, u, c]

    def other_unit(level, phase, slot, u):
        g = gathered[level][phase]
        return g.at[slot, 1 - c, u] if level == 0 else g.at[slot, u, 1 - c]

    def copy(level, phase, ref, index, peer):
        return pltpu.make_async_remote_copy(
            src_ref=ref,
            dst_ref=ref,
            send_sem=send_sem.at[level, phase, index],
            recv_sem=recv_sem.at[level, phase, index],
            device_id=peer,
            device_id_type=MESH,
        )

    def send(*args):
        copy(*args).start()

    def to_sibling(level, phase, rel, u):
        send(level, phase, unit(level, phase, slots[rel], u), SIBLING + 2 * rel + u, sibling)

    def send_unit(level, phase, u):
        ref = unit(level, phase, y, u)
        send(level, phase, ref, RIGHT + u, right)
        send(level, phase, ref, LEFT + u, left)
        to_sibling(level, phase, 0, u)

    def start(level, phase):
        if level == 0:
            first, second = unit(0, phase, y, 0), unit(0, phase, y, 1)
            send(0, phase, first, RIGHT, right)
            send(0, phase, second, LEFT + 1, left)
            send(0, phase, second, RIGHT + 1, right)
            send(0, phase, first, LEFT, left)
            to_sibling(0, phase, 0, 0)
            to_sibling(0, phase, 0, 1)
        else:
            mine = own_map(level)
            send(level, phase, unit(level, phase, y, mine), ACROSS, (pos ^ 2**level, y))
            send_unit(level, phase, mine)

    def across(level, phase):
        if level:
            theirs = 1 - own_map(level)
            ref = unit(level, phase, y, theirs)
            copy(level, phase, ref, ACROSS, (pos ^ 2**level, y)).wait_recv()
            send_unit(level, phase, theirs)

    def arrived(level, phase, rel, u, index):
        copy(level, phase, unit(level, phase, slots[rel], u), index, left).wait_recv()

    def forward(level, phase):
        arrived(level, phase, 1, 0, RIGHT)
        send(level, phase, unit(level, phase, slots[1], 0), ON_RIGHT, right)
        to_sibling(level, phase, 1, 0)
        arrived(level, phase, 2, 1, LEFT + 1)
        send(level, phase, unit(level, phase, slots[2], 1), ON_LEFT, left)
        to_sibling(level, phase, 2, 1)

    def near_rest(level, phase):
        arrived(level, phase, 1, 1, RIGHT + 1)
        to_sibling(level, phase, 1, 1)
        arrived(level, phase, 2, 0, LEFT)
        to_sibling(level, phase, 2, 0)

    def far(level, phase):
        arrived(level, phase, 3, 0, ON_RIGHT)
        to_sibling(level, phase, 3, 0)
        arrived(level, phase, 3, 1, ON_LEFT)
        to_sibling(level, phase, 3, 1)

    def convert(level, phase, rel):
        for u in range(2):
            ref = other_unit(level, phase, slots[rel], u)
            copy(level, phase, ref, SIBLING + 2 * rel + u, sibling).wait_recv()
        columns = pl.ds(pl.multiple_of(slots[rel] * BLK, BLK), BLK)
        g = gathered[level][phase]
        for m in range(2):
            for r in range(2):
                high, low = split(g[slots[rel], m, r])
                mats[level, 2 * phase + m, 0, r * HALF : (r + 1) * HALF, columns] = high
                mats[level, 2 * phase + m, 1, r * HALF : (r + 1) * HALF, columns] = low

    def rows_of(i):
        return pl.ds(pl.multiple_of(i * HALF, HALF), HALF)

    def product(a, b, finish):
        def half(i, carry):
            rows = rows_of(i)
            finish(rows, mm((a[0, rows, :], a[1, rows, :]), (b[0], b[1])))
            return carry

        lax.fori_loop(0, 2, half, 0)

    def keep(ref, rows, x):
        high, low = split(x)
        ref[0, rows, :] = high
        ref[1, rows, :] = low

    bit_y = bit_of(0, y)
    for k in range(4):
        bit = bit_of(0, k)
        even = leaf[0, 2 * k * BLK : (2 * k + 1) * BLK, :]
        odd = leaf[0, (2 * k + 1) * BLK : (2 * k + 2) * BLK, :]
        rows = slice(k % 2 * BLK, (k % 2 + 1) * BLK)
        near = pick(bit, odd, even)
        away = pick(bit, even, odd)
        g0i[y, c, k // 2, rows, :] = pick(bit_y, near[:, BLK:], near[:, :BLK])
        g0o[y, c, k // 2, rows, :] = pick(bit_y, near[:, :BLK], near[:, BLK:])
        dall[k // 2, rows, :] = pick(bit_y, away[:, :BLK], away[:, BLK:])
    ext[0, c] = dall[c]

    pl.semaphore_wait(barrier, 5)

    def ext_copy(level):
        return pltpu.make_async_remote_copy(
            src_ref=dall.at[1 - c] if level == 0 else ext.at[1, own_map(1)],
            dst_ref=ext.at[level, own_map(level)],
            send_sem=ext_send.at[level],
            recv_sem=ext_recv.at[level],
            device_id=(pos ^ 2**level, y),
            device_id_type=MESH,
        )

    for level in range(LEVELS):
        start(level, 0)
        across(level, 0)
        convert(level, 0, 0)
        forward(level, 0)
        near_rest(level, 0)
        start(level, 1)
        convert(level, 0, 1)
        convert(level, 0, 2)
        far(level, 0)
        if level < 2:
            ext_copy(level).start()
        convert(level, 0, 3)
        across(level, 1)

        alpha, beta, alpha_out, beta_out, coupling = (mats.at[level, i] for i in range(5))
        one, two, four, three = (work.at[i] for i in range(4))

        def first(rows, x):
            wf[0, rows, :] = x
            keep(one, rows, x)

        product(beta, alpha, first)

        def second(rows, x):
            wf[1, rows, :] = x
            keep(two, rows, x)

        product(one, one, second)
        forward(level, 1)

        def third(rows, x):
            shape = x.shape
            row = lax.broadcasted_iota(jnp.int32, shape, 0) + rows.start
            column = lax.broadcasted_iota(jnp.int32, shape, 1)
            x = x + wf[0, rows, :] + wf[1, rows, :] + jnp.where(row == column, 1.0, 0.0)
            wf[0, rows, :] = x
            keep(three, rows, x)

        product(one, two, third)
        near_rest(level, 1)
        product(two, two, lambda rows, x: keep(four, rows, x))
        convert(level, 1, 0)
        product(three, four, lambda rows, x: keep(coupling, rows, wf[0, rows, :] + x))

        if level < 2:
            mine = pl.ds(pl.multiple_of(y * BLK, BLK), BLK)

            def couple(i, carry):
                rows = rows_of(i)
                x = mm(
                    (beta[0, rows, :], beta[1, rows, :]),
                    (alpha_out[0, :, mine], alpha_out[1, :, mine]),
                )
                high, low = split(x)
                vs[0, rows, :BLK] = high
                vs[1, rows, :BLK] = low
                vs[0, rows, BLK:] = -beta_out[0, rows, mine]
                vs[1, rows, BLK:] = -beta_out[1, rows, mine]
                return carry

            lax.fori_loop(0, 2, couple, 0)
            far(level, 1)
            product(coupling, vs, lambda rows, x: keep(ss.at[0], rows, x))

            def back(i, carry):
                rows = rows_of(i)
                x = -mm((alpha[0, rows, :], alpha[1, rows, :]), (ss[0, 0], ss[0, 1]))
                own = gathered[level][1][y, 0, i]
                x = jnp.concatenate([x[:, :BLK] - own, x[:, BLK:]], 1)
                keep(ss.at[1], rows, x)
                return carry

            lax.fori_loop(0, 2, back, 0)
        else:
            far(level, 1)
        convert(level, 1, 1)
        convert(level, 1, 2)
        convert(level, 1, 3)

        if level < 2:
            ext_copy(level).wait_recv()
            above = level + 1
            bit_y = bit_of(above, y)
            outer = gathered[level][1]

            def merged(kk, chosen):
                k = 2 * c + kk
                bit = bit_of(above, k)
                part = bit if chosen else 1 - bit
                r = pick(part, outer[k, 1], outer[k, 0]).reshape(IFACE, BLK)
                x = mm(split(r.T), (ss[part, 0], ss[part, 1]))
                rows = slice(kk * BLK, (kk + 1) * BLK)
                kept = pick(part, ext[level, 1, rows, :], ext[level, 0, rows, :])
                return x[:, :BLK], x[:, BLK:], kept, part, rows

            for kk in range(2):
                lower, upper, kept, part, rows = merged(kk, True)
                lower = lower + pick(part, jnp.zeros_like(kept), kept)
                upper = upper + pick(part, kept, jnp.zeros_like(kept))
                gi, go = gathered[above]
                gi[y, own_map(above), c, rows, :] = pick(bit_y, upper, lower)
                go[y, own_map(above), c, rows, :] = pick(bit_y, lower, upper)
            if level == 0:
                for kk in range(2):
                    lower, upper, kept, part, rows = merged(kk, False)
                    lower = lower + pick(part, jnp.zeros_like(kept), kept)
                    upper = upper + pick(part, kept, jnp.zeros_like(kept))
                    ext[1, own_map(1), rows, :] = pick(bit_y, lower, upper)

    root_copy.wait()
    for level in reversed(range(LEVELS)):
        alpha, beta, alpha_out, beta_out, coupling = (mats.at[level, i] for i in range(5))
        for k in range(4):
            rows = slice(k * BLK, (k + 1) * BLK)
            keep(fs.at[0], rows, p[2 * k * BLK : (2 * k + 1) * BLK, :])
            keep(fs.at[1], rows, p[(2 * k + 1) * BLK : (2 * k + 2) * BLK, :])

        def through(rows, x):
            t32[0, rows, :] = x
            keep(ts, rows, x)

        product(alpha_out, fs.at[0], through)

        def feed(i, carry):
            rows = rows_of(i)
            x = mm((beta[0, rows, :], beta[1, rows, :]), (ts[0], ts[1]))
            x = x - mm((beta_out[0, rows, :], beta_out[1, rows, :]), (fs[1, 0], fs[1, 1]))
            keep(ds, rows, x)
            return carry

        lax.fori_loop(0, 2, feed, 0)

        def solve(rows, x):
            t32[1, rows, :] = x
            keep(ts, rows, x)

        product(coupling, ds, solve)

        upper_half = own_map(level)

        def close(rows, x):
            fb = -(t32[0, rows, :] + x)
            t32[0, rows, :] = pick(upper_half, fb, t32[1, rows, :])

        product(alpha, ts, close)
        target = p if level else out.at[0]
        for k in range(4):
            bit = bit_of(level, k)
            near = t32[0, k * BLK : (k + 1) * BLK, :]
            f1 = p[2 * k * BLK : (2 * k + 1) * BLK, :]
            f2 = p[(2 * k + 1) * BLK : (2 * k + 2) * BLK, :]
            away = pick(upper_half, f2, f1)
            target[2 * k * BLK : (2 * k + 1) * BLK, :] = pick(bit, away, near)
            target[(2 * k + 1) * BLK : (2 * k + 2) * BLK, :] = pick(bit, near, away)

    for level in range(LEVELS):
        for phase in range(2):
            if level:
                ref = unit(level, phase, y, own_map(level))
                copy(level, phase, ref, ACROSS, left).wait_send()
            for index in range(1, COPIES):
                copy(level, phase, unit(level, phase, y, 0), index, left).wait_send()
    for level in range(2):
        ext_copy(level).wait_send()


def shards(leaf_maps, interface_blocks, root_data):
    vmem = pl.BlockSpec(memory_space=pltpu.VMEM)
    units = pltpu.VMEM((4, 2, 2, HALF, BLK), F32)
    return pl.pallas_call(
        kernel,
        out_shape=jax.ShapeDtypeStruct((1,) + root_data.shape[1:], F32),
        in_specs=[
            pl.BlockSpec(memory_space=pltpu.SMEM),
            vmem,
            pl.BlockSpec(memory_space=pl.ANY),
        ],
        out_specs=vmem,
        scratch_shapes=[units] * 6
        + [
            pltpu.VMEM((LEVELS, 5, 2, IFACE, IFACE), BF16),
            pltpu.VMEM((4, 2, IFACE, IFACE), BF16),
            pltpu.VMEM((2, IFACE, IFACE), F32),
            pltpu.VMEM((2, IFACE, HALF), BF16),
            pltpu.VMEM((2, 2, IFACE, HALF), BF16),
            pltpu.VMEM((2, 2, HALF, BLK), F32),
            pltpu.VMEM((2, HALF, BLK), F32),
            pltpu.VMEM((2 * IFACE, BLK), F32),
            pltpu.VMEM((2, 2, IFACE, BLK), BF16),
            pltpu.VMEM((2, IFACE, BLK), F32),
            pltpu.VMEM((2, IFACE, BLK), BF16),
            pltpu.VMEM((2, IFACE, BLK), BF16),
            pltpu.SemaphoreType.DMA((LEVELS, 2, COPIES)),
            pltpu.SemaphoreType.DMA((LEVELS, 2, COPIES)),
            pltpu.SemaphoreType.DMA((2,)),
            pltpu.SemaphoreType.DMA((2,)),
            pltpu.SemaphoreType.DMA,
        ],
        compiler_params=pltpu.CompilerParams(
            collective_id=0, has_side_effects=True, vmem_limit_bytes=56 * 2**20
        ),
        name="merge_and_sweep",
    )(interface_blocks, leaf_maps, root_data)


def solution(mesh):
    return jax.shard_map(
        shards,
        mesh=mesh,
        in_specs=(P("box", None, "col"), P(), P(None, None, "col")),
        out_specs=P("box", None, "col"),
        check_vma=False,
    )
```

time: 524 us -> 105 us (0.20)
  waiting for transfers between devices: 232 us -> 0 us
  local copies, waits for them, and re-layouts: 115 us -> 3.31 us
  matrix products: 102 us -> 0 us
  Pallas kernels: 0 us -> 102 us
  other arithmetic: 45.3 us -> 0 us
  between operations: 17.4 us -> 0.01 us
  starting transfers between devices: 7.44 us -> 0 us
    all_gather x6 -> x0, waiting for transfers between devices: 163 us -> none  [the longest x3 83.4 us: shards(): lax.all_gather(beta_local, 'col', axis=1, tiled=True)]
    dot_general x48 -> x0, matrix products: 102 us -> none  [the longest x40 88.1 us: high_dot(): jnp.dot(left, right, precision=lax.Precision.HIGHEST, preferred_element_t...]
    pallas_call x0 -> x1, Pallas kernels: none -> 102 us  [shards(): pl.pallas_call(kernel, out_shape=jax.ShapeDtypeStruct((1,) + root_data.sh...]
    ppermute x3 -> x0, waiting for transfers between devices: 69.4 us -> none  [from_partner(): return lax.ppermute(block, axis, route)]
    gather x22 -> x0, local copies, waits for them, and re-layouts: 45.4 us -> none  [the longest x12 29.9 us: take_blocks(): return jnp.take(shaped, block_ids, axis=1).reshape(matrix.shape[0], -1)]
    select_n x29 -> x0, other arithmetic: 39.7 us -> none  [the longest x13 21.4 us: take_blocks(): return jnp.take(shaped, block_ids, axis=1).reshape(matrix.shape[0], -1)]
    select_n x12 -> x0, local copies, waits for them, and re-layouts: 25.5 us -> none  [take_blocks(): return jnp.take(shaped, block_ids, axis=1).reshape(matrix.shape[0], -1)]
    reshape x12 -> x0, local copies, waits for them, and re-layouts: 25.4 us -> none  [the longest x6 16.3 us: take_blocks(): matrix.reshape(matrix.shape[0], matrix.shape[1] // block_width, block_width)]
  transfers between devices with their start and end apart: 9 -> 0, of which waited for: 9 -> 0; matrix products, arithmetic and copies ran while one was open for 9% -> 0% of each run, Pallas kernels for 0% -> 0%
where the time goes in v1:
time: 105 us
  Pallas kernels  102 us (97%)
  local copies, waits for them, and re-layouts  3.31 us (3%)
    pallas_call x1, Pallas kernels, shards(): pl.pallas_call(kernel, out_shape=jax.ShapeDtypeStruct((1,) + root_data.sh...  102 us
    unnamed x2, local copies, waits for them, and re-layouts  3.31 us

profile of v1, /device:TPU:1, one launch (start us, length us, event | category | flops | bytes accessed | tf_op | source)
XLA Modules:
  0.0 104.8 jit_solution(10384005283185243313)
XLA Ops:
  0.0 1.4 %copy.4.table = s32[3,64,4]{2,1,0:T(8,128)} copy(s32[3,64,4]{1,2,0:T(4,128)} %param.4) | data formatting | bytes 6144 | tf_op args[1]
  1.4 101.5 %merge_and_sweep.1 = f32[1,1024,128]{2,1,0:T(8,128)} custom-call(s32[3,64,4]{2,1,0:T(8,128)} %copy.4.table, f32[1,1024,256]{2,1,0:T(8,128)} %leaf.1, f32[8,1024,128]{2,1,0:T(8,128)} %root.1), custom_call_target="tpu_custom_call" | custom-call | tf_op jit(solution)/shard_map/merge_and_sweep/pallas_call | solution.py:358
  103.0 1.9 %copy.6 = f32[1,1024,128]{2,1,0:T(8,128)} copy(f32[1,1024,128]{2,1,0:T(8,128)} %merge_and_sweep.1) | data formatting | bytes 1048576

commit v2 on v1

v2 whole, which is shorter than its diff:
```python
import functools

import jax
import jax.numpy as jnp
from jax import lax
from jax.experimental import pallas as pl
from jax.experimental.pallas import tpu as pltpu
from jax.sharding import PartitionSpec as P

LEVELS = 3
IFACE = 512
BLK = 128
HALF = 256
F32 = jnp.float32
BF16 = jnp.bfloat16
MESH = pl.DeviceIdType.MESH

ACROSS, RIGHT, LEFT, FAR, SIBLING, BESIDE, COPIES = 0, 1, 3, 5, 7, 15, 23


def split(x):
    high = x.astype(BF16)
    return high, (x - high.astype(F32)).astype(BF16)


def mm(a, b):
    dot = functools.partial(jnp.dot, preferred_element_type=F32)
    return dot(a[0], b[0]) + (dot(a[0], b[1]) + dot(a[1], b[0]))


def pick(flag, yes, no):
    return jnp.where(jnp.broadcast_to(flag, yes.shape) == 1, yes, no)


def kernel(
    table, leaf, root, out,
    g0i, g0o, g1i, g1o, g2i, g2o,
    raw, both, down, mats, work, wf, vs, vf, ss, ext, dall, p, fs, t32, ts, ds,
    send_sem, recv_sem, ext_send, ext_recv, root_sem,
):
    pos = lax.axis_index("box")
    y = lax.axis_index("col")
    c = pos % 2
    gathered = ((g0i, g0o), (g1i, g1o), (g2i, g2o))
    slots = (y, (y + 3) % 4, (y + 1) % 4, (y + 2) % 4)
    right, left, opposite, sibling = (pos, slots[2]), (pos, slots[1]), (pos, slots[3]), (pos ^ 1, y)

    root_copy = pltpu.make_async_copy(root.at[pos // 8], p, root_sem)
    root_copy.start()

    barrier = pltpu.get_barrier_semaphore()
    for peer in (right, left, opposite, sibling, (pos ^ 2, y), (pos ^ 4, y)):
        pl.semaphore_signal(barrier, inc=1, device_id=peer, device_id_type=MESH)

    def own_map(level):
        return (pos >> level) & 1

    def bit_of(level, k):
        return table[level, pos - pos % 2**level, k] & 1

    def next_bit(level, k):
        return bit_of(level + 1, k) if level + 1 < LEVELS else jnp.int32(0)

    def unit(level, phase, slot, u):
        g = gathered[level][phase]
        return g.at[slot, c, u] if level + phase == 0 else g.at[slot, u, c]

    def copy(level, phase, ref, index, peer, src=None):
        return pltpu.make_async_remote_copy(
            src_ref=ref if src is None else src,
            dst_ref=ref,
            send_sem=send_sem.at[level, phase, index],
            recv_sem=recv_sem.at[level, phase, index],
            device_id=peer,
            device_id_type=MESH,
        )

    def send(*args):
        copy(*args).start()

    z_low = (pos >> 1) & 1
    beside = (pos ^ 2, y)

    def half(ref, which):
        return ref.at[pl.ds(pl.multiple_of(which * BLK, BLK), BLK)]

    def to_beside(level, phase, rel, u):
        ref = half(unit(level, phase, slots[rel], u), z_low)
        send(level, phase, ref, BESIDE + 2 * rel + u, beside)

    def split_around(level, phase, u):
        ref = half(unit(level, phase, y, u), z_low)
        send(level, phase, ref, RIGHT + u, right)
        send(level, phase, ref, LEFT + u, left)
        send(level, phase, ref, FAR + u, opposite)

    def serve_split(level, phase, u):
        for rel in (1, 2, 3):
            ref = half(unit(level, phase, slots[rel], u), z_low)
            copy(level, phase, ref, (0, RIGHT, LEFT, FAR)[rel] + u, left).wait_recv()
            to_beside(level, phase, rel, u)

    def join_split(level, phase, u, rels=(1, 2, 3)):
        for rel in rels:
            ref = half(unit(level, phase, slots[rel], u), 1 - z_low)
            copy(level, phase, ref, BESIDE + 2 * rel + u, beside).wait_recv()
            to_sibling(level, phase, rel, u)

    def to_sibling(level, phase, rel, u):
        send(level, phase, unit(level, phase, slots[rel], u), SIBLING + 2 * rel + u, sibling)

    def from_sibling(level, phase, rel, u):
        ref = unit(level, phase, slots[rel], u)
        copy(level, phase, ref, SIBLING + 2 * rel + u, sibling).wait_recv()

    def send_next(level, phase, u):
        ref = unit(level, phase, y, u)
        send(level, phase, ref, RIGHT + u, right)
        send(level, phase, ref, LEFT + u, left)

    def send_far(level, phase, u):
        send(level, phase, unit(level, phase, y, u), FAR + u, opposite)

    def send_around(level, phase, u):
        send_next(level, phase, u)
        send_far(level, phase, u)

    def sent(level, phase, u, kinds):
        ref = unit(level, phase, y, u)
        for index in kinds:
            copy(level, phase, ref, index + u, right).wait_send()

    def arrived(level, phase, rel, u):
        index = (0, RIGHT, LEFT, FAR)[rel] + u
        copy(level, phase, unit(level, phase, slots[rel], u), index, left).wait_recv()

    def relay_far(level):
        mine = own_map(level)
        ref = unit(level, 0, slots[3], mine)
        pltpu.make_async_remote_copy(
            src_ref=ref,
            dst_ref=ref,
            send_sem=send_sem.at[level, 0, FAR + 1 - mine],
            recv_sem=recv_sem.at[level, 0, FAR + mine],
            device_id=(pos ^ 2**level, y),
            device_id_type=MESH,
        ).start()

    def serve(level, phase, u, rels=(1, 2, 3)):
        for rel in rels:
            arrived(level, phase, rel, u)
            to_sibling(level, phase, rel, u)

    def columns_of(rel):
        return pl.ds(pl.multiple_of(slots[rel] * BLK, BLK), BLK)

    def rows_of(i):
        return pl.ds(pl.multiple_of(i * HALF, HALF), HALF)

    def keep(ref, rows, x, columns=slice(None)):
        high, low = split(x)
        ref[0, rows, columns] = high
        ref[1, rows, columns] = low

    def keep_inner(level, rel, m):
        for r in range(2):
            x = gathered[level][0][slots[rel], m, r]
            keep(mats.at[level, m], slice(r * HALF, (r + 1) * HALF), x, columns_of(rel))

    def keep_outer(level, rel, awaited=(0, 1)):
        for q in awaited:
            from_sibling(level, 1, rel, q)
        bit = next_bit(level, slots[rel])
        g = gathered[level][1]
        for r in range(2):
            rows = slice(r * HALF, (r + 1) * HALF)
            chosen, rest = g[slots[rel], 0, r], g[slots[rel], 1, r]
            keep(mats.at[level, 2], rows, pick(bit, rest, chosen), columns_of(rel))
            keep(mats.at[level, 3], rows, pick(bit, chosen, rest), columns_of(rel))

    def pair(ref):
        return ref[0], ref[1]

    everything = slice(None)

    def order_outer(level):
        theirs = 1 - own_map(level)
        copy(level, 1, raw.at[level, theirs], ACROSS, sibling).wait_recv()
        bit = next_bit(level, y)
        g = gathered[level][1]
        g[y, 0, c] = pick(bit, raw[level, 1], raw[level, 0])
        g[y, 1, c] = pick(bit, raw[level, 0], raw[level, 1])
        to_sibling(level, 1, 0, 0)
        to_sibling(level, 1, 0, 1)

    def finish_cubes(level):
        one, two, four, three = (work.at[i] for i in range(4))
        x = mm(pair(one), pair(two)) + wf[0] + wf[1]
        row = lax.broadcasted_iota(jnp.int32, x.shape, 0)
        column = lax.broadcasted_iota(jnp.int32, x.shape, 1)
        x = x + jnp.where(row == column, 1.0, 0.0)
        wf[0] = x
        keep(three, everything, x)
        keep(four, everything, mm(pair(two), pair(two)))

    def finish_coupling(level):
        keep(mats.at[level, 4], everything, wf[0] + mm(pair(work.at[3]), pair(work.at[2])))

    def sweep_operator(level):
        alpha, beta, alpha_out, beta_out, coupling = (mats.at[level, i] for i in range(5))
        x = mm(pair(beta), pair(alpha_out))
        keep(work.at[0], everything, x)
        keep(work.at[1], everything, mm(pair(coupling), pair(work.at[0])))
        keep(work.at[2], everything, -mm(pair(coupling), pair(beta_out)))
        upper_half = own_map(level)
        for i in range(2):
            near = work.at[1 + i]
            x = -mm(pair(alpha), pair(near))
            if i == 0:
                x = x - (alpha_out[0].astype(F32) + alpha_out[1].astype(F32))
            held = near[0].astype(F32) + near[1].astype(F32)
            columns = slice(i * IFACE, (i + 1) * IFACE)
            keep(down.at[level], everything, pick(upper_half, x, held), columns)

    def ext_copy(level):
        return pltpu.make_async_remote_copy(
            src_ref=dall.at[1 - c] if level == 0 else ext.at[1, own_map(1)],
            dst_ref=ext.at[level, own_map(level)],
            send_sem=ext_send.at[level],
            recv_sem=ext_recv.at[level],
            device_id=(pos ^ 2**level, y),
            device_id_type=MESH,
        )

    def merged(level, kk, rest):
        k = 2 * c + kk
        bit = bit_of(level + 1, k)
        part = 1 - bit if rest else bit
        r = gathered[level][1][k, rest].reshape(IFACE, BLK)
        x = mm(split(r.T), (ss[part, 0], ss[part, 1]))
        rows = slice(kk * BLK, (kk + 1) * BLK)
        kept = pick(part, ext[level, 1, rows, :], ext[level, 0, rows, :])
        lower = x[:, :BLK] + pick(part, jnp.zeros_like(kept), kept)
        upper = x[:, BLK:] + pick(part, kept, jnp.zeros_like(kept))
        return lower, upper, rows

    bit_y = bit_of(0, y)
    for k in range(4):
        bit = bit_of(0, k)
        even = leaf[0, 2 * k * BLK : (2 * k + 1) * BLK, :]
        odd = leaf[0, (2 * k + 1) * BLK : (2 * k + 2) * BLK, :]
        rows = slice(k % 2 * BLK, (k % 2 + 1) * BLK)
        near = pick(bit, odd, even)
        away = pick(bit, even, odd)
        g0i[y, c, k // 2, rows, :] = pick(bit_y, near[:, BLK:], near[:, :BLK])
        both[k // 2, rows, :] = pick(bit_y, near[:, :BLK], near[:, BLK:])
        dall[k // 2, rows, :] = pick(bit_y, away[:, :BLK], away[:, BLK:])

    pl.semaphore_wait(barrier, 6)

    for level in range(LEVELS):
        alpha, beta, alpha_out, beta_out, coupling = (mats.at[level, i] for i in range(5))
        one, two, four, three = (work.at[i] for i in range(4))
        mine = own_map(level)
        if level == 0:
            first, second = unit(0, 0, y, 0), unit(0, 0, y, 1)
            send(0, 0, first, RIGHT, right)
            send(0, 0, second, LEFT + 1, left)
            send(0, 0, second, RIGHT + 1, right)
            send(0, 0, first, LEFT, left)
            to_sibling(0, 0, 0, 0)
            to_sibling(0, 0, 0, 1)
            send(0, 1, raw.at[0, mine], ACROSS, sibling, both.at[1 - c])
            ext_copy(0).start()
            raw[0, mine] = both[c]
            ext[0, mine] = dall[c]
            order_outer(0)
            for u in range(2):
                from_sibling(0, 0, 0, u)
            keep_inner(0, 0, 0)
            keep_inner(0, 0, 1)
            arrived(0, 0, 1, 0)
            send(0, 0, unit(0, 0, slots[1], 0), FAR, right)
            to_sibling(0, 0, 1, 0)
            arrived(0, 0, 2, 1)
            send(0, 0, unit(0, 0, slots[2], 1), FAR + 1, left)
            to_sibling(0, 0, 2, 1)
            keep_outer(0, 0)
            arrived(0, 0, 1, 1)
            to_sibling(0, 0, 1, 1)
            arrived(0, 0, 2, 0)
            to_sibling(0, 0, 2, 0)
            send_around(0, 1, 0)
            for rel in (1, 2):
                for u in range(2):
                    from_sibling(0, 0, rel, u)
                keep_inner(0, rel, 0)
                keep_inner(0, rel, 1)
            for u in range(2):
                arrived(0, 0, 3, u)
                to_sibling(0, 0, 3, u)
            for u in range(2):
                from_sibling(0, 0, 3, u)
            keep_inner(0, 3, 0)
            keep_inner(0, 3, 1)
        else:
            theirs = 1 - mine
            last = level == LEVELS - 1
            partner = (pos ^ 2**level, y)
            if last:
                send(level, 0, half(unit(level, 0, y, mine), z_low), ACROSS, partner)
                split_around(level, 0, mine)
                to_sibling(level, 0, 0, mine)
                send(level, 1, unit(level, 1, y, mine), ACROSS, partner)
                to_sibling(level, 1, 0, mine)
                finish_cubes(level - 1)
                serve_split(level - 1, 1, 1)
                send_next(level, 1, mine)
                ref = half(unit(level, 0, y, theirs), z_low)
                copy(level, 0, ref, ACROSS, partner).wait_recv()
                split_around(level, 0, theirs)
                to_beside(level, 0, 0, theirs)
                serve_split(level, 0, mine)
                finish_coupling(level - 1)
                join_split(level - 1, 1, 1)
                join_split(level, 0, theirs, (0,))
                for rel in range(1, 4):
                    keep_outer(level - 1, rel, (1,))
                send_far(level, 1, mine)
                join_split(level, 0, mine)
                serve_split(level, 0, theirs)
                copy(level, 1, unit(level, 1, y, theirs), ACROSS, partner).wait_recv()
                to_sibling(level, 1, 0, theirs)
                send_around(level, 1, theirs)
                for rel in range(4):
                    from_sibling(level, 0, rel, mine)
                    keep_inner(level, rel, mine)
                keep_outer(level, 0)
                sweep_operator(1)
                join_split(level, 0, theirs)
                for rel in range(4):
                    from_sibling(level, 0, rel, theirs)
                    keep_inner(level, rel, theirs)
            else:
                send(level, 0, unit(level, 0, y, mine), ACROSS, partner)
                send_around(level, 0, mine)
                to_sibling(level, 0, 0, mine)
                send(level, 1, raw.at[level, mine], ACROSS, partner)
                finish_cubes(level - 1)
                copy(level, 0, unit(level, 0, y, theirs), ACROSS, partner).wait_recv()
                send_next(level, 0, theirs)
                to_sibling(level, 0, 0, theirs)
                order_outer(level)
                serve(level - 1, 1, 1)
                serve(level, 0, mine)
                relay_far(level)
                finish_coupling(level - 1)
                for rel in range(1, 4):
                    keep_outer(level - 1, rel, (1,))
                bit_y = bit_of(1, y)
                for kk in range(2):
                    lower, upper, rows = merged(0, kk, 1)
                    ext[1, mine, rows, :] = pick(bit_y, lower, upper)
                ext_copy(1).start()
                sent(level, 0, theirs, (RIGHT, LEFT))
                send_around(level, 1, 0)
                for rel in range(4):
                    from_sibling(level, 0, rel, mine)
                    keep_inner(level, rel, mine)
                keep_outer(level, 0)
                serve(level, 0, theirs, (1, 2))
                sweep_operator(0)
                for rel in range(3):
                    from_sibling(level, 0, rel, theirs)
                    keep_inner(level, rel, theirs)
                serve(level, 0, theirs, (3,))
                from_sibling(level, 0, 3, theirs)
                keep_inner(level, 3, theirs)

        if level == LEVELS - 1:
            x = mm(pair(beta), pair(alpha))
            wf[0] = x
            keep(one, everything, x)
            serve(level, 1, mine)
            x = mm(pair(one), pair(one))
            wf[1] = x
            keep(two, everything, x)
            finish_cubes(level)
            finish_coupling(level)
            serve(level, 1, theirs)
            for rel in range(1, 4):
                keep_outer(level, rel)
            break

        own = columns_of(0)
        bit = next_bit(level, y)
        x = mm(
            pair(beta),
            [jnp.concatenate([alpha[i], alpha_out[i, :, own]], 1) for i in range(2)],
        )
        wf[0] = x[:, :IFACE]
        keep(one, everything, x[:, :IFACE])
        vf[:, :BLK] = x[:, IFACE:]
        for r in range(2):
            chosen, rest = gathered[level][1][y, 0, r], gathered[level][1][y, 1, r]
            vf[r * HALF : (r + 1) * HALF, BLK:] = -pick(bit, chosen, rest)
        keep(vs, everything, vf[...])
        x = mm(pair(one), [jnp.concatenate([one[i], vs[i]], 1) for i in range(2)])
        wf[1] = x[:, :IFACE]
        keep(two, everything, x[:, :IFACE])
        x = vf[...] + x[:, IFACE:]
        vf[...] = x
        keep(vs, everything, x)
        (send_around if level == 0 else split_around)(level, 1, 1)
        x = vf[...] + mm(pair(two), pair(vs))
        vf[...] = x
        keep(vs, everything, x)
        keep(vs, everything, mm(pair(two), pair(vs)))
        serve(level, 1, 0)
        x = vf[...] + mm(pair(two), pair(vs))
        keep(ss.at[0], everything, x)
        x = -mm(pair(alpha), pair(ss.at[0]))
        for r in range(2):
            rows = slice(r * HALF, (r + 1) * HALF)
            chosen, rest = gathered[level][1][y, 0, r], gathered[level][1][y, 1, r]
            keep(ss.at[1], rows, x[rows, :BLK] - pick(bit, rest, chosen), slice(0, BLK))
            keep(ss.at[1], rows, x[rows, BLK:], slice(BLK, HALF))
        for rel in range(1, 4):
            from_sibling(level, 1, rel, 0)
        ext_copy(level).wait_recv()
        above = level + 1
        bit_y = bit_of(above, y)
        for kk in range(2):
            lower, upper, rows = merged(level, kk, 0)
            gathered[above][0][y, own_map(above), c, rows, :] = pick(bit_y, upper, lower)
            outer = pick(bit_y, lower, upper)
            if above == LEVELS - 1:
                gathered[above][1][y, own_map(above), c, rows, :] = outer
            else:
                raw[above, own_map(above), rows, :] = outer

    root_copy.wait()
    for level in reversed(range(LEVELS)):
        alpha, beta, alpha_out, beta_out, coupling = (mats.at[level, i] for i in range(5))
        upper_half = own_map(level)
        for k in range(8):
            rows = slice((k % 2 * 4 + k // 2) * BLK, (k % 2 * 4 + k // 2 + 1) * BLK)
            keep(fs, rows, p[k * BLK : (k + 1) * BLK, :])
        if level == LEVELS - 1:
            first, second = slice(0, IFACE), slice(IFACE, 2 * IFACE)
            x = mm(pair(alpha_out), (fs[0, first], fs[1, first]))
            t32[0] = x
            keep(ts, everything, x)
            x = mm(pair(beta), pair(ts)) - mm(pair(beta_out), (fs[0, second], fs[1, second]))
            keep(ds, everything, x)
            x = mm(pair(coupling), pair(ds))
            t32[1] = x
            keep(ts, everything, x)
            x = mm(pair(alpha), pair(ts))
            t32[0] = pick(upper_half, -(t32[0] + x), t32[1])
        else:
            t32[0] = mm(pair(down.at[level]), pair(fs))
        target = p if level else out.at[0]
        for k in range(4):
            bit = bit_of(level, k)
            near = t32[0, k * BLK : (k + 1) * BLK, :]
            f1 = p[2 * k * BLK : (2 * k + 1) * BLK, :]
            f2 = p[(2 * k + 1) * BLK : (2 * k + 2) * BLK, :]
            away = pick(upper_half, f2, f1)
            target[2 * k * BLK : (2 * k + 1) * BLK, :] = pick(bit, away, near)
            target[(2 * k + 1) * BLK : (2 * k + 2) * BLK, :] = pick(bit, near, away)

    for level in range(LEVELS):
        mine = own_map(level)
        for phase in range(2):
            whole = unit(level, phase, y, 0)
            parted = half(whole, 0)
            inner_top = level == LEVELS - 1 and not phase
            if level + phase:
                copy(level, phase, parted if inner_top else whole, ACROSS, left).wait_send()
            for index in range(SIBLING, BESIDE):
                copy(level, phase, whole, index, left).wait_send()
            if inner_top:
                for index in range(RIGHT, SIBLING):
                    copy(level, phase, parted, index, left).wait_send()
                for index in range(BESIDE + 2, COPIES):
                    copy(level, phase, parted, index, left).wait_send()
                copy(level, phase, parted, BESIDE + 1 - mine, left).wait_send()
            elif level == 1 and phase:
                sent(level, phase, 0, (RIGHT, LEFT, FAR))
                for rel in range(1, 4):
                    copy(level, phase, parted, BESIDE + 2 * rel + 1, left).wait_send()
                for index in (RIGHT, LEFT, FAR):
                    copy(level, phase, parted, index + 1, left).wait_send()
            elif level == 1:
                sent(level, 0, mine, (RIGHT, LEFT, FAR))
                sent(level, 0, 1 - mine, (FAR,))
            else:
                for u in range(2):
                    sent(level, phase, u, (RIGHT, LEFT, FAR))
    for level in range(2):
        ext_copy(level).wait_send()


def shards(leaf_maps, interface_blocks, root_data):
    vmem = pl.BlockSpec(memory_space=pltpu.VMEM)
    units = pltpu.VMEM((4, 2, 2, HALF, BLK), F32)
    return pl.pallas_call(
        kernel,
        out_shape=jax.ShapeDtypeStruct((1,) + root_data.shape[1:], F32),
        in_specs=[
            pl.BlockSpec(memory_space=pltpu.SMEM),
            vmem,
            pl.BlockSpec(memory_space=pl.ANY),
        ],
        out_specs=vmem,
        scratch_shapes=[units] * 6
        + [
            pltpu.VMEM((LEVELS, 2, HALF, BLK), F32),
            pltpu.VMEM((2, HALF, BLK), F32),
            pltpu.VMEM((2, 2, IFACE, 2 * IFACE), BF16),
            pltpu.VMEM((LEVELS, 5, 2, IFACE, IFACE), BF16),
            pltpu.VMEM((4, 2, IFACE, IFACE), BF16),
            pltpu.VMEM((2, IFACE, IFACE), F32),
            pltpu.VMEM((2, IFACE, HALF), BF16),
            pltpu.VMEM((IFACE, HALF), F32),
            pltpu.VMEM((2, 2, IFACE, HALF), BF16),
            pltpu.VMEM((2, 2, HALF, BLK), F32),
            pltpu.VMEM((2, HALF, BLK), F32),
            pltpu.VMEM((2 * IFACE, BLK), F32),
            pltpu.VMEM((2, 2 * IFACE, BLK), BF16),
            pltpu.VMEM((2, IFACE, BLK), F32),
            pltpu.VMEM((2, IFACE, BLK), BF16),
            pltpu.VMEM((2, IFACE, BLK), BF16),
            pltpu.SemaphoreType.DMA((LEVELS, 2, COPIES)),
            pltpu.SemaphoreType.DMA((LEVELS, 2, COPIES)),
            pltpu.SemaphoreType.DMA((2,)),
            pltpu.SemaphoreType.DMA((2,)),
            pltpu.SemaphoreType.DMA,
        ],
        compiler_params=pltpu.CompilerParams(
            collective_id=0, has_side_effects=True, vmem_limit_bytes=56 * 2**20
        ),
        name="merge_and_sweep",
    )(interface_blocks, leaf_maps, root_data)


def solution(mesh):
    return jax.shard_map(
        shards,
        mesh=mesh,
        in_specs=(P("box", None, "col"), P(), P(None, None, "col")),
        out_specs=P("box", None, "col"),
        check_vma=False,
    )
```

time: 105 us -> 104 us (level)
  Pallas kernels: 102 us -> 100 us
    pallas_call x1, Pallas kernels: 102 us -> 100 us  [shards(): pl.pallas_call(kernel, out_shape=jax.ShapeDtypeStruct((1,) + root_data.sh...]
where the time goes in v2:
time: 104 us; the launch traced here: 103 us
  Pallas kernels  100 us (96%)
  local copies, waits for them, and re-layouts  3.31 us (3%)
    pallas_call x1, Pallas kernels, shards(): pl.pallas_call(kernel, out_shape=jax.ShapeDtypeStruct((1,) + root_data.sh...  100 us
    unnamed x2, local copies, waits for them, and re-layouts  3.31 us

profile of v2, /device:TPU:1, one launch (start us, length us, event | category | flops | bytes accessed | tf_op | source)
XLA Modules:
  0.0 103.5 jit_solution(12968755741930259330)
XLA Ops:
  0.0 1.4 %copy.4.table = s32[3,64,4]{2,1,0:T(8,128)} copy(s32[3,64,4]{1,2,0:T(4,128)} %param.4) | data formatting | bytes 6144 | tf_op args[1]
  1.4 100.1 %merge_and_sweep.1 = f32[1,1024,128]{2,1,0:T(8,128)} custom-call(s32[3,64,4]{2,1,0:T(8,128)} %copy.4.table, f32[1,1024,256]{2,1,0:T(8,128)} %leaf.1, f32[8,1024,128]{2,1,0:T(8,128)} %root.1), custom_call_target="tpu_custom_call" | custom-call | tf_op jit(solution)/shard_map/merge_and_sweep/pallas_call | solution.py:508
  101.6 1.9 %copy.6 = f32[1,1024,128]{2,1,0:T(8,128)} copy(f32[1,1024,128]{2,1,0:T(8,128)} %merge_and_sweep.1) | data formatting | bytes 1048576

commit v3 on v2

--- a/solution.py
+++ b/solution.py
@@ -28,6 +28,13 @@
     return dot(a[0], b[0]) + (dot(a[0], b[1]) + dot(a[1], b[0]))
 
 
+def mm_nt(a, b):
+    dot = functools.partial(
+        lax.dot_general, dimension_numbers=(((1,), (1,)), ((), ())), preferred_element_type=F32
+    )
+    return dot(a[0], b[0]) + (dot(a[0], b[1]) + dot(a[1], b[0]))
+
+
 def pick(flag, yes, no):
     return jnp.where(jnp.broadcast_to(flag, yes.shape) == 1, yes, no)
 
@@ -35,7 +42,7 @@
 def kernel(
     table, leaf, root, out,
     g0i, g0o, g1i, g1o, g2i, g2o,
-    raw, both, down, mats, work, wf, vs, vf, ss, ext, dall, p, fs, t32, ts, ds,
+    raw, both, down, mats, work, wf, vs, vf, ss, ext, dall, pr, p, fs, t32, ts, ds,
     send_sem, recv_sem, ext_send, ext_recv, root_sem,
 ):
     pos = lax.axis_index("box")
@@ -45,7 +52,7 @@
     slots = (y, (y + 3) % 4, (y + 1) % 4, (y + 2) % 4)
     right, left, opposite, sibling = (pos, slots[2]), (pos, slots[1]), (pos, slots[3]), (pos ^ 1, y)
 
-    root_copy = pltpu.make_async_copy(root.at[pos // 8], p, root_sem)
+    root_copy = pltpu.make_async_copy(root.at[pos // 8], pr, root_sem)
     root_copy.start()
 
     barrier = pltpu.get_barrier_semaphore()
@@ -82,7 +89,7 @@
     beside = (pos ^ 2, y)
 
     def half(ref, which):
-        return ref.at[pl.ds(pl.multiple_of(which * BLK, BLK), BLK)]
+        return ref.at[which]
 
     def to_beside(level, phase, rel, u):
         ref = half(unit(level, phase, slots[rel], u), z_low)
@@ -151,11 +158,11 @@
             arrived(level, phase, rel, u)
             to_sibling(level, phase, rel, u)
 
-    def columns_of(rel):
+    def rows_of(rel):
         return pl.ds(pl.multiple_of(slots[rel] * BLK, BLK), BLK)
 
-    def rows_of(i):
-        return pl.ds(pl.multiple_of(i * HALF, HALF), HALF)
+    def block(k):
+        return slice(k * BLK, (k + 1) * BLK)
 
     def keep(ref, rows, x, columns=slice(None)):
         high, low = split(x)
@@ -163,20 +170,19 @@
         ref[1, rows, columns] = low
 
     def keep_inner(level, rel, m):
-        for r in range(2):
-            x = gathered[level][0][slots[rel], m, r]
-            keep(mats.at[level, m], slice(r * HALF, (r + 1) * HALF), x, columns_of(rel))
+        for k in range(4):
+            x = gathered[level][0][slots[rel], m, k // 2, k % 2]
+            keep(mats.at[level, m], rows_of(rel), x, block(k))
 
     def keep_outer(level, rel, awaited=(0, 1)):
         for q in awaited:
             from_sibling(level, 1, rel, q)
         bit = next_bit(level, slots[rel])
         g = gathered[level][1]
-        for r in range(2):
-            rows = slice(r * HALF, (r + 1) * HALF)
-            chosen, rest = g[slots[rel], 0, r], g[slots[rel], 1, r]
-            keep(mats.at[level, 2], rows, pick(bit, rest, chosen), columns_of(rel))
-            keep(mats.at[level, 3], rows, pick(bit, chosen, rest), columns_of(rel))
+        for k in range(4):
+            chosen, rest = g[slots[rel], 0, k // 2, k % 2], g[slots[rel], 1, k // 2, k % 2]
+            keep(mats.at[level, 2], rows_of(rel), pick(bit, rest, chosen), block(k))
+            keep(mats.at[level, 3], rows_of(rel), pick(bit, chosen, rest), block(k))
 
     def pair(ref):
         return ref[0], ref[1]
@@ -208,19 +214,21 @@
 
     def sweep_operator(level):
         alpha, beta, alpha_out, beta_out, coupling = (mats.at[level, i] for i in range(5))
-        x = mm(pair(beta), pair(alpha_out))
+        x = mm(pair(alpha_out), pair(beta))
         keep(work.at[0], everything, x)
-        keep(work.at[1], everything, mm(pair(coupling), pair(work.at[0])))
-        keep(work.at[2], everything, -mm(pair(coupling), pair(beta_out)))
+        keep(down.at[level], slice(0, IFACE), mm(pair(work.at[0]), pair(coupling)))
+        keep(down.at[level], slice(IFACE, 2 * IFACE), -mm(pair(beta_out), pair(coupling)))
+
+    def sweep_operator_beta(level):
         upper_half = own_map(level)
         for i in range(2):
-            near = work.at[1 + i]
-            x = -mm(pair(alpha), pair(near))
+            rows = slice(i * IFACE, (i + 1) * IFACE)
+            near = (down[level, 0, rows, :], down[level, 1, rows, :])
+            x = -mm(near, pair(mats.at[level, 0]))
             if i == 0:
-                x = x - (alpha_out[0].astype(F32) + alpha_out[1].astype(F32))
+                x = x - (mats[level, 2, 0].astype(F32) + mats[level, 2, 1].astype(F32))
             held = near[0].astype(F32) + near[1].astype(F32)
-            columns = slice(i * IFACE, (i + 1) * IFACE)
-            keep(down.at[level], everything, pick(upper_half, x, held), columns)
+            keep(down.at[level], rows, pick(upper_half, x, held))
 
     def ext_copy(level):
         return pltpu.make_async_remote_copy(
@@ -236,25 +244,24 @@
         k = 2 * c + kk
         bit = bit_of(level + 1, k)
         part = 1 - bit if rest else bit
-        r = gathered[level][1][k, rest].reshape(IFACE, BLK)
-        x = mm(split(r.T), (ss[part, 0], ss[part, 1]))
-        rows = slice(kk * BLK, (kk + 1) * BLK)
-        kept = pick(part, ext[level, 1, rows, :], ext[level, 0, rows, :])
-        lower = x[:, :BLK] + pick(part, jnp.zeros_like(kept), kept)
-        upper = x[:, BLK:] + pick(part, kept, jnp.zeros_like(kept))
-        return lower, upper, rows
+        g = gathered[level][1]
+        r = split(jnp.concatenate([g[k, rest, i // 2, i % 2] for i in range(4)], 1))
+        x = mm_nt((ss[part, 0], ss[part, 1]), r)
+        kept = pick(part, ext[level, 1, kk], ext[level, 0, kk])
+        lower = x[:BLK] + pick(part, jnp.zeros_like(kept), kept)
+        upper = x[BLK:] + pick(part, kept, jnp.zeros_like(kept))
+        return lower, upper
 
     bit_y = bit_of(0, y)
     for k in range(4):
         bit = bit_of(0, k)
         even = leaf[0, 2 * k * BLK : (2 * k + 1) * BLK, :]
         odd = leaf[0, (2 * k + 1) * BLK : (2 * k + 2) * BLK, :]
-        rows = slice(k % 2 * BLK, (k % 2 + 1) * BLK)
-        near = pick(bit, odd, even)
-        away = pick(bit, even, odd)
-        g0i[y, c, k // 2, rows, :] = pick(bit_y, near[:, BLK:], near[:, :BLK])
-        both[k // 2, rows, :] = pick(bit_y, near[:, :BLK], near[:, BLK:])
-        dall[k // 2, rows, :] = pick(bit_y, away[:, :BLK], away[:, BLK:])
+        near = pick(bit, odd, even).T
+        away = pick(bit, even, odd).T
+        g0i[y, c, k // 2, k % 2] = pick(bit_y, near[BLK:], near[:BLK])
+        both[k // 2, k % 2] = pick(bit_y, near[:BLK], near[BLK:])
+        dall[k // 2, k % 2] = pick(bit_y, away[:BLK], away[BLK:])
 
     pl.semaphore_wait(barrier, 6)
 
@@ -315,19 +322,20 @@
                 to_sibling(level, 1, 0, mine)
                 finish_cubes(level - 1)
                 serve_split(level - 1, 1, 1)
+                finish_coupling(level - 1)
                 send_next(level, 1, mine)
                 ref = half(unit(level, 0, y, theirs), z_low)
                 copy(level, 0, ref, ACROSS, partner).wait_recv()
                 split_around(level, 0, theirs)
                 to_beside(level, 0, 0, theirs)
                 serve_split(level, 0, mine)
-                finish_coupling(level - 1)
                 join_split(level - 1, 1, 1)
                 join_split(level, 0, theirs, (0,))
                 for rel in range(1, 4):
                     keep_outer(level - 1, rel, (1,))
                 send_far(level, 1, mine)
                 join_split(level, 0, mine)
+                sweep_operator(1)
                 serve_split(level, 0, theirs)
                 copy(level, 1, unit(level, 1, y, theirs), ACROSS, partner).wait_recv()
                 to_sibling(level, 1, 0, theirs)
@@ -336,7 +344,7 @@
                     from_sibling(level, 0, rel, mine)
                     keep_inner(level, rel, mine)
                 keep_outer(level, 0)
-                sweep_operator(1)
+                sweep_operator_beta(1)
                 join_split(level, 0, theirs)
                 for rel in range(4):
                     from_sibling(level, 0, rel, theirs)
@@ -359,17 +367,21 @@
                     keep_outer(level - 1, rel, (1,))
                 bit_y = bit_of(1, y)
                 for kk in range(2):
-                    lower, upper, rows = merged(0, kk, 1)
-                    ext[1, mine, rows, :] = pick(bit_y, lower, upper)
+                    lower, upper = merged(0, kk, 1)
+                    ext[1, mine, kk] = pick(bit_y, lower, upper)
                 ext_copy(1).start()
                 sent(level, 0, theirs, (RIGHT, LEFT))
                 send_around(level, 1, 0)
+                sweep_operator(0)
+                root_copy.wait()
+                for k in range(8):
+                    p[k] = pr[block(k), :].T
                 for rel in range(4):
                     from_sibling(level, 0, rel, mine)
                     keep_inner(level, rel, mine)
                 keep_outer(level, 0)
                 serve(level, 0, theirs, (1, 2))
-                sweep_operator(0)
+                sweep_operator_beta(0)
                 for rel in range(3):
                     from_sibling(level, 0, rel, theirs)
                     keep_inner(level, rel, theirs)
@@ -378,7 +390,7 @@
                 keep_inner(level, 3, theirs)
 
         if level == LEVELS - 1:
-            x = mm(pair(beta), pair(alpha))
+            x = mm(pair(alpha), pair(beta))
             wf[0] = x
             keep(one, everything, x)
             serve(level, 1, mine)
@@ -392,83 +404,83 @@
                 keep_outer(level, rel)
             break
 
-        own = columns_of(0)
+        own = rows_of(0)
         bit = next_bit(level, y)
+        g = gathered[level][1]
         x = mm(
+            [jnp.concatenate([alpha[i], alpha_out[i, own, :]], 0) for i in range(2)],
             pair(beta),
-            [jnp.concatenate([alpha[i], alpha_out[i, :, own]], 1) for i in range(2)],
         )
-        wf[0] = x[:, :IFACE]
-        keep(one, everything, x[:, :IFACE])
-        vf[:, :BLK] = x[:, IFACE:]
-        for r in range(2):
-            chosen, rest = gathered[level][1][y, 0, r], gathered[level][1][y, 1, r]
-            vf[r * HALF : (r + 1) * HALF, BLK:] = -pick(bit, chosen, rest)
+        wf[0] = x[:IFACE]
+        keep(one, everything, x[:IFACE])
+        vf[:BLK, :] = x[IFACE:]
+        for k in range(4):
+            chosen, rest = g[y, 0, k // 2, k % 2], g[y, 1, k // 2, k % 2]
+            vf[BLK:, block(k)] = -pick(bit, chosen, rest)
         keep(vs, everything, vf[...])
-        x = mm(pair(one), [jnp.concatenate([one[i], vs[i]], 1) for i in range(2)])
-        wf[1] = x[:, :IFACE]
-        keep(two, everything, x[:, :IFACE])
-        x = vf[...] + x[:, IFACE:]
+        x = mm([jnp.concatenate([one[i], vs[i]], 0) for i in range(2)], pair(one))
+        wf[1] = x[:IFACE]
+        keep(two, everything, x[:IFACE])
+        x = vf[...] + x[IFACE:]
         vf[...] = x
         keep(vs, everything, x)
         (send_around if level == 0 else split_around)(level, 1, 1)
-        x = vf[...] + mm(pair(two), pair(vs))
+        x = vf[...] + mm(pair(vs), pair(two))
         vf[...] = x
         keep(vs, everything, x)
-        keep(vs, everything, mm(pair(two), pair(vs)))
+        keep(vs, everything, mm(pair(vs), pair(two)))
         serve(level, 1, 0)
-        x = vf[...] + mm(pair(two), pair(vs))
+        x = vf[...] + mm(pair(vs), pair(two))
         keep(ss.at[0], everything, x)
-        x = -mm(pair(alpha), pair(ss.at[0]))
-        for r in range(2):
-            rows = slice(r * HALF, (r + 1) * HALF)
-            chosen, rest = gathered[level][1][y, 0, r], gathered[level][1][y, 1, r]
-            keep(ss.at[1], rows, x[rows, :BLK] - pick(bit, rest, chosen), slice(0, BLK))
-            keep(ss.at[1], rows, x[rows, BLK:], slice(BLK, HALF))
+        x = -mm(pair(ss.at[0]), pair(alpha))
+        keep(ss.at[1], slice(BLK, HALF), x[BLK:])
+        for k in range(4):
+            chosen, rest = g[y, 0, k // 2, k % 2], g[y, 1, k // 2, k % 2]
+            keep(ss.at[1], slice(0, BLK), x[:BLK, block(k)] - pick(bit, rest, chosen), block(k))
         for rel in range(1, 4):
             from_sibling(level, 1, rel, 0)
         ext_copy(level).wait_recv()
         above = level + 1
         bit_y = bit_of(above, y)
         for kk in range(2):
-            lower, upper, rows = merged(level, kk, 0)
-            gathered[above][0][y, own_map(above), c, rows, :] = pick(bit_y, upper, lower)
+            lower, upper = merged(level, kk, 0)
+            gathered[above][0][y, own_map(above), c, kk] = pick(bit_y, upper, lower)
             outer = pick(bit_y, lower, upper)
             if above == LEVELS - 1:
-                gathered[above][1][y, own_map(above), c, rows, :] = outer
+                gathered[above][1][y, own_map(above), c, kk] = outer
             else:
-                raw[above, own_map(above), rows, :] = outer
-
-    root_copy.wait()
+                raw[above, own_map(above), kk] = outer
+
     for level in reversed(range(LEVELS)):
         alpha, beta, alpha_out, beta_out, coupling = (mats.at[level, i] for i in range(5))
         upper_half = own_map(level)
         for k in range(8):
-            rows = slice((k % 2 * 4 + k // 2) * BLK, (k % 2 * 4 + k // 2 + 1) * BLK)
-            keep(fs, rows, p[k * BLK : (k + 1) * BLK, :])
+            keep(fs, everything, p[k], block(k % 2 * 4 + k // 2))
         if level == LEVELS - 1:
             first, second = slice(0, IFACE), slice(IFACE, 2 * IFACE)
-            x = mm(pair(alpha_out), (fs[0, first], fs[1, first]))
+            x = mm((fs[0, :, first], fs[1, :, first]), pair(alpha_out))
             t32[0] = x
             keep(ts, everything, x)
-            x = mm(pair(beta), pair(ts)) - mm(pair(beta_out), (fs[0, second], fs[1, second]))
+            x = mm(pair(ts), pair(beta)) - mm((fs[0, :, second], fs[1, :, second]), pair(beta_out))
             keep(ds, everything, x)
-            x = mm(pair(coupling), pair(ds))
+            x = mm(pair(ds), pair(coupling))
             t32[1] = x
             keep(ts, everything, x)
-            x = mm(pair(alpha), pair(ts))
+            x = mm(pair(ts), pair(alpha))
             t32[0] = pick(upper_half, -(t32[0] + x), t32[1])
         else:
-            t32[0] = mm(pair(down.at[level]), pair(fs))
-        target = p if level else out.at[0]
+            t32[0] = mm(pair(fs), pair(down.at[level]))
         for k in range(4):
             bit = bit_of(level, k)
-            near = t32[0, k * BLK : (k + 1) * BLK, :]
-            f1 = p[2 * k * BLK : (2 * k + 1) * BLK, :]
-            f2 = p[(2 * k + 1) * BLK : (2 * k + 2) * BLK, :]
-            away = pick(upper_half, f2, f1)
-            target[2 * k * BLK : (2 * k + 1) * BLK, :] = pick(bit, away, near)
-            target[(2 * k + 1) * BLK : (2 * k + 2) * BLK, :] = pick(bit, near, away)
+            near = t32[0, :, block(k)]
+            away = pick(upper_half, p[2 * k + 1], p[2 * k])
+            even, odd = pick(bit, away, near), pick(bit, near, away)
+            if level:
+                p[2 * k] = even
+                p[2 * k + 1] = odd
+            else:
+                out[0, block(2 * k), :] = even.T
+                out[0, block(2 * k + 1), :] = odd.T
 
     for level in range(LEVELS):
         mine = own_map(level)
@@ -504,7 +516,7 @@
 
 def shards(leaf_maps, interface_blocks, root_data):
     vmem = pl.BlockSpec(memory_space=pltpu.VMEM)
-    units = pltpu.VMEM((4, 2, 2, HALF, BLK), F32)
+    units = pltpu.VMEM((4, 2, 2, 2, BLK, BLK), F32)
     return pl.pallas_call(
         kernel,
         out_shape=jax.ShapeDtypeStruct((1,) + root_data.shape[1:], F32),
@@ -516,22 +528,23 @@
         out_specs=vmem,
         scratch_shapes=[units] * 6
         + [
-            pltpu.VMEM((LEVELS, 2, HALF, BLK), F32),
-            pltpu.VMEM((2, HALF, BLK), F32),
-            pltpu.VMEM((2, 2, IFACE, 2 * IFACE), BF16),
+            pltpu.VMEM((LEVELS, 2, 2, BLK, BLK), F32),
+            pltpu.VMEM((2, 2, BLK, BLK), F32),
+            pltpu.VMEM((2, 2, 2 * IFACE, IFACE), BF16),
             pltpu.VMEM((LEVELS, 5, 2, IFACE, IFACE), BF16),
             pltpu.VMEM((4, 2, IFACE, IFACE), BF16),
             pltpu.VMEM((2, IFACE, IFACE), F32),
-            pltpu.VMEM((2, IFACE, HALF), BF16),
-            pltpu.VMEM((IFACE, HALF), F32),
-            pltpu.VMEM((2, 2, IFACE, HALF), BF16),
-            pltpu.VMEM((2, 2, HALF, BLK), F32),
-            pltpu.VMEM((2, HALF, BLK), F32),
+            pltpu.VMEM((2, HALF, IFACE), BF16),
+            pltpu.VMEM((HALF, IFACE), F32),
+            pltpu.VMEM((2, 2, HALF, IFACE), BF16),
+            pltpu.VMEM((2, 2, 2, BLK, BLK), F32),
+            pltpu.VMEM((2, 2, BLK, BLK), F32),
             pltpu.VMEM((2 * IFACE, BLK), F32),
-            pltpu.VMEM((2, 2 * IFACE, BLK), BF16),
-            pltpu.VMEM((2, IFACE, BLK), F32),
-            pltpu.VMEM((2, IFACE, BLK), BF16),
-            pltpu.VMEM((2, IFACE, BLK), BF16),
+            pltpu.VMEM((8, BLK, BLK), F32),
+            pltpu.VMEM((2, BLK, 2 * IFACE), BF16),
+            pltpu.VMEM((2, BLK, IFACE), F32),
+            pltpu.VMEM((2, BLK, IFACE), BF16),
+            pltpu.VMEM((2, BLK, IFACE), BF16),
             pltpu.SemaphoreType.DMA((LEVELS, 2, COPIES)),
             pltpu.SemaphoreType.DMA((LEVELS, 2, COPIES)),
             pltpu.SemaphoreType.DMA((2,)),

time: 104 us -> 94.9 us (0.913)
  Pallas kernels: 100 us -> 91.4 us
    pallas_call x1, Pallas kernels: 100 us -> 91.4 us  [shards(): pl.pallas_call(kernel, out_shape=jax.ShapeDtypeStruct((1,) + root_data.sh...]
where the time goes in v3:
time: 94.9 us; the launch traced here: 94.7 us
  Pallas kernels  91.4 us (96%)
  local copies, waits for them, and re-layouts  3.31 us (3%)
    pallas_call x1, Pallas kernels, shards(): pl.pallas_call(kernel, out_shape=jax.ShapeDtypeStruct((1,) + root_data.sh...  91.4 us
    unnamed x2, local copies, waits for them, and re-layouts  3.31 us

profile of v3, /device:TPU:1, one launch (start us, length us, event | category | flops | bytes accessed | tf_op | source)
XLA Modules:
  0.0 94.7 jit_solution(11705013302624402865)
XLA Ops:
  0.0 1.4 %copy.4.table = s32[3,64,4]{2,1,0:T(8,128)} copy(s32[3,64,4]{1,2,0:T(4,128)} %param.4) | data formatting | bytes 6144 | tf_op args[1]
  1.4 91.4 %merge_and_sweep.1 = f32[1,1024,128]{2,1,0:T(8,128)} custom-call(s32[3,64,4]{2,1,0:T(8,128)} %copy.4.table, f32[1,1024,256]{2,1,0:T(8,128)} %leaf.1, f32[8,1024,128]{2,1,0:T(8,128)} %root.1), custom_call_target="tpu_custom_call" | custom-call | tf_op jit(solution)/shard_map/merge_and_sweep/pallas_call | solution.py:520
  92.8 1.9 %copy.6 = f32[1,1024,128]{2,1,0:T(8,128)} copy(f32[1,1024,128]{2,1,0:T(8,128)} %merge_and_sweep.1) | data formatting | bytes 1048576

commit v4 on v3

--- a/solution.py
+++ b/solution.py
@@ -63,7 +63,7 @@
         return (pos >> level) & 1
 
     def bit_of(level, k):
-        return table[level, pos - pos % 2**level, k] & 1
+        return table[level, k, pos - pos % 2**level] & 1
 
     def next_bit(level, k):
         return bit_of(level + 1, k) if level + 1 < LEVELS else jnp.int32(0)
@@ -322,8 +322,9 @@
                 to_sibling(level, 1, 0, mine)
                 finish_cubes(level - 1)
                 serve_split(level - 1, 1, 1)
+                send_next(level, 1, mine)
+                sweep_operator_beta(0)
                 finish_coupling(level - 1)
-                send_next(level, 1, mine)
                 ref = half(unit(level, 0, y, theirs), z_low)
                 copy(level, 0, ref, ACROSS, partner).wait_recv()
                 split_around(level, 0, theirs)
@@ -335,11 +336,11 @@
                     keep_outer(level - 1, rel, (1,))
                 send_far(level, 1, mine)
                 join_split(level, 0, mine)
-                sweep_operator(1)
                 serve_split(level, 0, theirs)
                 copy(level, 1, unit(level, 1, y, theirs), ACROSS, partner).wait_recv()
                 to_sibling(level, 1, 0, theirs)
                 send_around(level, 1, theirs)
+                sweep_operator(1)
                 for rel in range(4):
                     from_sibling(level, 0, rel, mine)
                     keep_inner(level, rel, mine)
@@ -381,7 +382,6 @@
                     keep_inner(level, rel, mine)
                 keep_outer(level, 0)
                 serve(level, 0, theirs, (1, 2))
-                sweep_operator_beta(0)
                 for rel in range(3):
                     from_sibling(level, 0, rel, theirs)
                     keep_inner(level, rel, theirs)
@@ -397,8 +397,6 @@
             x = mm(pair(one), pair(one))
             wf[1] = x
             keep(two, everything, x)
-            finish_cubes(level)
-            finish_coupling(level)
             serve(level, 1, theirs)
             for rel in range(1, 4):
                 keep_outer(level, rel)
@@ -463,7 +461,12 @@
             keep(ts, everything, x)
             x = mm(pair(ts), pair(beta)) - mm((fs[0, :, second], fs[1, :, second]), pair(beta_out))
             keep(ds, everything, x)
-            x = mm(pair(ds), pair(coupling))
+            one, two = work.at[0], work.at[1]
+            for factor in (one, two):
+                x = x + mm(pair(ds), pair(factor))
+                keep(ds, everything, x)
+            keep(ds, everything, mm(pair(ds), pair(two)))
+            x = x + mm(pair(ds), pair(two))
             t32[1] = x
             keep(ts, everything, x)
             x = mm(pair(ts), pair(alpha))
@@ -555,7 +558,7 @@
             collective_id=0, has_side_effects=True, vmem_limit_bytes=56 * 2**20
         ),
         name="merge_and_sweep",
-    )(interface_blocks, leaf_maps, root_data)
+    )(interface_blocks.transpose(0, 2, 1), leaf_maps, root_data)
 
 
 def solution(mesh):

time: 94.9 us -> 87.8 us (0.925)
  Pallas kernels: 91.4 us -> 85.8 us
  local copies, waits for them, and re-layouts: 3.31 us -> 1.87 us
    pallas_call x1, Pallas kernels: 91.4 us -> 85.8 us  [shards(): pl.pallas_call(kernel, out_shape=jax.ShapeDtypeStruct((1,) + root_data.sh...]
    unnamed x2 -> x1, local copies, waits for them, and re-layouts: 3.31 us -> 1.87 us
where the time goes in v4:
time: 87.8 us; the launch traced here: 87.7 us
  Pallas kernels  85.8 us (98%)
  local copies, waits for them, and re-layouts  1.87 us (2%)
    pallas_call x1, Pallas kernels, shards(): pl.pallas_call(kernel, out_shape=jax.ShapeDtypeStruct((1,) + root_data.sh...  85.8 us
    unnamed x1, local copies, waits for them, and re-layouts  1.87 us

profile of v4, /device:TPU:1, one launch (start us, length us, event | category | flops | bytes accessed | tf_op | source)
XLA Modules:
  0.0 87.7 jit_solution(13820833004833904862)
XLA Ops:
  0.0 85.8 %merge_and_sweep.1 = f32[1,1024,128]{2,1,0:T(8,128)} custom-call(s32[3,4,64]{2,1,0:T(4,128)} %bitcast.1, f32[1,1024,256]{2,1,0:T(8,128)} %leaf.1, f32[8,1024,128]{2,1,0:T(8,128)} %root.1), custom_call_target="tpu_custom_call" | custom-call | tf_op jit(solution)/shard_map/merge_and_sweep/pallas_call | solution.py:523
  85.8 1.9 %copy.5 = f32[1,1024,128]{2,1,0:T(8,128)} copy(f32[1,1024,128]{2,1,0:T(8,128)} %merge_and_sweep.1) | data formatting | bytes 1048576

commit v5 on v4

--- a/solution.py
+++ b/solution.py
@@ -345,11 +345,17 @@
                     from_sibling(level, 0, rel, mine)
                     keep_inner(level, rel, mine)
                 keep_outer(level, 0)
-                sweep_operator_beta(1)
-                join_split(level, 0, theirs)
                 for rel in range(4):
-                    from_sibling(level, 0, rel, theirs)
-                    keep_inner(level, rel, theirs)
+                    if rel:
+                        join_split(level, 0, theirs, (rel,))
+                    if rel > 1:
+                        from_sibling(level, 0, rel - 1, theirs)
+                        keep_inner(level, rel - 1, theirs)
+                    elif rel == 1:
+                        from_sibling(level, 0, 0, theirs)
+                        keep_inner(level, 0, theirs)
+                from_sibling(level, 0, 3, theirs)
+                keep_inner(level, 3, theirs)
             else:
                 send(level, 0, unit(level, 0, y, mine), ACROSS, partner)
                 send_around(level, 0, mine)
@@ -359,11 +365,11 @@
                 copy(level, 0, unit(level, 0, y, theirs), ACROSS, partner).wait_recv()
                 send_next(level, 0, theirs)
                 to_sibling(level, 0, 0, theirs)
+                serve(level - 1, 1, 1)
                 order_outer(level)
-                serve(level - 1, 1, 1)
+                finish_coupling(level - 1)
                 serve(level, 0, mine)
                 relay_far(level)
-                finish_coupling(level - 1)
                 for rel in range(1, 4):
                     keep_outer(level - 1, rel, (1,))
                 bit_y = bit_of(1, y)
@@ -373,6 +379,7 @@
                 ext_copy(1).start()
                 sent(level, 0, theirs, (RIGHT, LEFT))
                 send_around(level, 1, 0)
+                serve(level, 0, theirs, (1, 2))
                 sweep_operator(0)
                 root_copy.wait()
                 for k in range(8):
@@ -381,7 +388,6 @@
                     from_sibling(level, 0, rel, mine)
                     keep_inner(level, rel, mine)
                 keep_outer(level, 0)
-                serve(level, 0, theirs, (1, 2))
                 for rel in range(3):
                     from_sibling(level, 0, rel, theirs)
                     keep_inner(level, rel, theirs)
@@ -472,7 +478,12 @@
             x = mm(pair(ts), pair(alpha))
             t32[0] = pick(upper_half, -(t32[0] + x), t32[1])
         else:
-            t32[0] = mm(pair(fs), pair(down.at[level]))
+            x = mm(pair(fs), pair(down.at[level]))
+            if level:
+                keep(ts, everything, x)
+                through = mm((fs[0, :, :IFACE], fs[1, :, :IFACE]), pair(alpha_out))
+                x = pick(upper_half, -(through + mm(pair(ts), pair(alpha))), x)
+            t32[0] = x
         for k in range(4):
             bit = bit_of(level, k)
             near = t32[0, :, block(k)]

time: 87.8 us -> 87.6 us (level)
  no operation moved by 1% of the time
where the time goes in v5:
time: 87.6 us; the launch traced here: 87.4 us
  Pallas kernels  85.5 us (98%)
  local copies, waits for them, and re-layouts  1.87 us (2%)
    pallas_call x1, Pallas kernels, shards(): pl.pallas_call(kernel, out_shape=jax.ShapeDtypeStruct((1,) + root_data.sh...  85.5 us
    unnamed x1, local copies, waits for them, and re-layouts  1.87 us

profile of v5, /device:TPU:1, one launch (start us, length us, event | category | flops | bytes accessed | tf_op | source)
XLA Modules:
  0.0 87.4 jit_solution(10897690486730400239)
XLA Ops:
  0.0 85.5 %merge_and_sweep.1 = f32[1,1024,128]{2,1,0:T(8,128)} custom-call(s32[3,4,64]{2,1,0:T(4,128)} %bitcast.1, f32[1,1024,256]{2,1,0:T(8,128)} %leaf.1, f32[8,1024,128]{2,1,0:T(8,128)} %root.1), custom_call_target="tpu_custom_call" | custom-call | tf_op jit(solution)/shard_map/merge_and_sweep/pallas_call | solution.py:534
  85.6 1.9 %copy.5 = f32[1,1024,128]{2,1,0:T(8,128)} copy(f32[1,1024,128]{2,1,0:T(8,128)} %merge_and_sweep.1) | data formatting | bytes 1048576
